TPU v7x, 32 devices: a whole 2x2x4 slice. The times are simulated.
32 devices in a mesh: group: 4 (over z), shard: 8 (over y, x, core).
Axes of the slice: x: 2, y: 2, z: 4, core: 2. Of those that a mesh axis runs over, the one named last changes fastest.
Arguments:
- entry_grads: float32 [4, 8, 256, 1280], P('group', 'shard'), may hold values from -800 to 800
- exit_grads: float32 [4, 8, 256, 1024], P('group', 'shard'), may hold values from -800 to 800
- entry_params: float32 [8, 256, 1280], P('shard', 'group'), may hold values from -0.15625 to 0.15625
- exit_params: float32 [8, 256, 1024], P('shard', 'group'), may hold values from -0.15625 to 0.15625
- entry_mean: float32 [8, 256, 1280], P('shard', 'group'), may hold values from -1.5 to 1.5
- exit_mean: float32 [8, 256, 1024], P('shard', 'group'), may hold values from -1.5 to 1.5
- entry_square: float32 [8, 256, 1280], P('shard', 'group'), may hold values from 0.01 to 1
- exit_square: float32 [8, 256, 1024], P('shard', 'group'), may hold values from 0.01 to 1
Outputs:
- entry_master: float32 [8, 256, 1280], P('shard', 'group')
- exit_master: float32 [8, 256, 1024], P('shard', 'group')
- entry_moment: float32 [8, 256, 1280], P('shard', 'group')
- exit_moment: float32 [8, 256, 1024], P('shard', 'group')
- entry_variance: float32 [8, 256, 1280], P('shard', 'group')
- exit_variance: float32 [8, 256, 1024], P('shard', 'group')
- entry_weights: bfloat16 [8, 256, 1280], P('shard')
- exit_weights: bfloat16 [8, 256, 1024], P('shard')
All inputs are finite; a program needn't handle non-finite values.
Results may differ from a plain program's by a relative error of at most 0.0004.
Values may be sent and summed in bfloat16 or wider, within the bound.
A program may use at most 64 MiB of HBM per device.

v0:
```python
import jax
import jax.numpy as jnp
from jax import lax
from jax.sharding import PartitionSpec as P

beta_first = 0.9
beta_second = 0.95
learn_rate = 0.01
decay_rate = 0.1
epsilon = 1e-08
correct_first = 1.0 - 0.9**40
correct_second = 1.0 - 0.95**40


def adamw_step(params, mean, square, total, clip):
    grads = clip * total
    moment = beta_first * mean + (1.0 - beta_first) * grads
    variance = beta_second * square + (1.0 - beta_second) * grads * grads
    update = moment / correct_first / (jnp.sqrt(variance / correct_second) + epsilon)
    master = params - learn_rate * (update + decay_rate * params)
    return (master, moment, variance)


def body(
    entry_grads,
    exit_grads,
    entry_params,
    exit_params,
    entry_mean,
    exit_mean,
    entry_square,
    exit_square,
):
    entry_rows_dev = entry_grads.shape[2]
    exit_rows_dev = exit_grads.shape[2]
    entry_width = entry_grads.shape[3]
    exit_width = exit_grads.shape[3]
    entry_local = entry_grads.reshape(entry_rows_dev, entry_width)
    exit_local = exit_grads.reshape(exit_rows_dev, exit_width)
    entry_total, exit_total = (
        lax.psum_scatter(entry_local, "group", scatter_dimension=0, tiled=True),
        lax.psum_scatter(exit_local, "group", scatter_dimension=0, tiled=True),
    )
    partial_value = jnp.sum(entry_total * entry_total) + jnp.sum(exit_total * exit_total)
    squares = lax.psum(partial_value, ("group", "shard"))
    count = (entry_rows_dev * entry_width + exit_rows_dev * exit_width) * lax.axis_size("shard")
    limit = jnp.sqrt(jnp.float32(count))
    clip = jnp.minimum(jnp.float32(1.0), limit / (jnp.sqrt(squares) + 1e-06))
    entry_master, entry_moment, entry_variance = adamw_step(
        entry_params[0], entry_mean[0], entry_square[0], entry_total, clip
    )
    exit_master, exit_moment, exit_variance = adamw_step(
        exit_params[0], exit_mean[0], exit_square[0], exit_total, clip
    )
    entry_round = entry_master.astype(jnp.bfloat16)
    exit_round = exit_master.astype(jnp.bfloat16)
    entry_weights = lax.all_gather(entry_round, "group", axis=0, tiled=True)
    exit_weights = lax.all_gather(exit_round, "group", axis=0, tiled=True)
    return (
        entry_master[None],
        exit_master[None],
        entry_moment[None],
        exit_moment[None],
        entry_variance[None],
        exit_variance[None],
        entry_weights[None],
        exit_weights[None],
    )


def solution(mesh):
    placed = (
        P("group", "shard", None, None),
        P("group", "shard", None, None),
        P("shard", "group", None),
        P("shard", "group", None),
        P("shard", "group", None),
        P("shard", "group", None),
        P("shard", "group", None),
        P("shard", "group", None),
    )
    return jax.shard_map(
        body,
        mesh=mesh,
        in_specs=placed,
        out_specs=(
            P("shard", "group", None),
            P("shard", "group", None),
            P("shard", "group", None),
            P("shard", "group", None),
            P("shard", "group", None),
            P("shard", "group", None),
            P("shard", None, None),
            P("shard", None, None),
        ),
        check_vma=False,
    )
```

profile of v0, /device:TPU:0, one launch (start us, length us, event | category | flops | bytes accessed | tf_op | source)
XLA Modules:
  0.0 158.2 jit_solution(12106391381337871409)
XLA Ops:
  7.2 0.0 reduce-scatter.5.cloned.1.call-start
  7.2 0.0 copy-start.1
  7.2 0.0 copy-start.2
  7.2 0.0 copy-start.3
  7.2 0.7 reduce-scatter.5.cloned.1.call-update
  7.9 0.0 reduce-scatter.3.cloned.1.call-start
  7.9 0.7 reduce-scatter.3.cloned.1.call-update
  8.7 31.5 %reduce-scatter.5.cloned.1.call-done = f32[64,1024]{1,0:T(8,128)} async-done(((f32[256,1024]{1,0:T(8,128)}), f32[64,1024]{1,0:T(8,128)}) %reduce-scatter.5.cloned.1.call-update) | async-done | bytes 262160 | tf_op jit(solution)/shard_map/reduce_scatter | solution.py:42
  40.2 1.6 %multiply_reduce_fusion.1 = f32[]{:T(128)} fusion(f32[64,1024]{1,0:T(8,128)} %reduce-scatter.5.cloned.1.call-done), kind=kLoop, calls=%fused_computation.15 | loop fusion | flops 131071 | bytes 262148 | tf_op jit(solution)/shard_map/reduce_sum | solution.py:44
  41.8 30.7 %reduce-scatter.3.cloned.1.call-done = f32[64,1280]{1,0:T(8,128)} async-done(((f32[256,1280]{1,0:T(8,128)}), f32[64,1280]{1,0:T(8,128)}) %reduce-scatter.3.cloned.1.call-update) | async-done | bytes 327696 | tf_op jit(solution)/shard_map/reduce_scatter | solution.py:41
  72.5 1.7 %multiply_reduce_fusion = f32[]{:T(128)} fusion(f32[64,1280]{1,0:T(8,128)} %reduce-scatter.3.cloned.1.call-done), kind=kLoop, calls=%fused_computation.8 | loop fusion | flops 163839 | bytes 327684 | tf_op jit(solution)/shard_map/reduce_sum | solution.py:44
  75.5 39.0 %psum.7 = f32[]{:T(128)} all-reduce(f32[]{:T(128)S(6)} %add.42), channel_id=1, replica_groups=mesh['group'=4,'shard'=8] {'group','shard'}, use_global_device_ids=true, to_apply=%region_4.0 | all-reduce | flops 1 | bytes 8 | tf_op jit(solution)/shard_map/psum | solution.py:45
  115.2 0.0 copy-done.1
  115.3 0.0 copy-start.4
  115.3 0.0 copy-start.5
  115.3 0.0 copy-start.6
  115.3 2.2 %fusion.11 = (bf16[64,1280]{1,0:T(8,128)(2,1)S(1)}, f32[64,1280]{1,0:T(8,128)}, f32[1,64,1280]{2,1,0:T(8,128)}, f32[1,64,1280]{2,1,0:T(8,128)}) fusion(f32[1,64,1280]{2,1,0:T(8,128)S(1)} %copy-done.1, f32[64,1280]{1,0:T(8,128)} %reduce-scatter.3.cloned.1.call-done, f32[]{:T(128)S(6)} %min_shard_map.3, f32[1,64,1280]{2,1,0:T(8,128)S(1)} %copy-done.2, ...), kind=kLoop, calls=%fused_computation.21 | loop fusion | flops 1392640 | bytes 2457604 | tf_op jit(solution)/shard_map/convert_element_type | solution.py:55
  117.4 16.4 %all_gather.6 = bf16[256,1280]{1,0:T(8,128)(2,1)S(1)} all-gather(bf16[64,1280]{1,0:T(8,128)(2,1)S(1)} %get-tuple-element.10), channel_id=1, replica_groups=mesh['group'=4,'shard'=8] {'group'}, dimensions={0}, use_global_device_ids=true | all-gather | bytes 819200 | tf_op jit(solution)/shard_map/all_gather | solution.py:57
  133.8 0.0 copy-done
  133.8 0.0 copy-done.5
  133.8 1.0 fusion.10
  134.8 14.9 %all_gather.7 = bf16[256,1024]{1,0:T(8,128)(2,1)S(1)} all-gather(bf16[64,1024]{1,0:T(8,128)(2,1)S(1)} %get-tuple-element.8), channel_id=1, replica_groups=mesh['group'=4,'shard'=8] {'group'}, dimensions={0}, use_global_device_ids=true | all-gather | bytes 655360 | tf_op jit(solution)/shard_map/all_gather | solution.py:58
  149.7 0.8 copy.18
  150.6 0.8 copy.19
  (5 shorter events, 0.0 us)
Async XLA Ops:
  7.2 33.0 %reduce-scatter.5.cloned.1.call-start = ((), (), s32[]{:S(2)}) async-start(), calls=%async_computation.3 | async-start | bytes 1310720 | tf_op jit(solution)/shard_map/reduce_scatter | solution.py:42
  7.2 108.0 %copy-start.1 = (f32[1,64,1280]{2,1,0:T(8,128)S(1)}, f32[1,64,1280]{2,1,0:T(8,128)}, u32[]{:S(2)}) copy-start(f32[1,64,1280]{2,1,0:T(8,128)} %param.14) | copy-start | bytes 983044
  7.2 108.0 %copy-start.2 = (f32[1,64,1280]{2,1,0:T(8,128)S(1)}, f32[1,64,1280]{2,1,0:T(8,128)}, u32[]{:S(2)}) copy-start(f32[1,64,1280]{2,1,0:T(8,128)} %param.12) | copy-start | bytes 983044
  7.2 108.0 %copy-start.3 = (f32[1,64,1280]{2,1,0:T(8,128)S(1)}, f32[1,64,1280]{2,1,0:T(8,128)}, u32[]{:S(2)}) copy-start(f32[1,64,1280]{2,1,0:T(8,128)} %param.10) | copy-start | bytes 983044
  7.9 64.6 %reduce-scatter.3.cloned.1.call-start = ((), (), s32[]{:S(2)}) async-start(), calls=%async_computation.2 | async-start | bytes 1638400 | tf_op jit(solution)/shard_map/reduce_scatter | solution.py:41
  115.2 18.6 %copy-start = (f32[64,1024]{1,0:T(8,128)S(1)}, f32[64,1024]{1,0:T(8,128)}, u32[]{:S(2)}) copy-start(f32[64,1024]{1,0:T(8,128)} %reduce-scatter.5.cloned.1.call-done) | copy-start | bytes 786436
  115.3 18.6 %copy-start.4 = (f32[1,64,1024]{2,1,0:T(8,128)S(1)}, f32[1,64,1024]{2,1,0:T(8,128)}, u32[]{:S(2)}) copy-start(f32[1,64,1024]{2,1,0:T(8,128)} %param.15) | copy-start | bytes 786436
  115.3 18.5 %copy-start.5 = (f32[1,64,1024]{2,1,0:T(8,128)S(1)}, f32[1,64,1024]{2,1,0:T(8,128)}, u32[]{:S(2)}) copy-start(f32[1,64,1024]{2,1,0:T(8,128)} %param.13) | copy-start | bytes 786436
  115.3 18.5 %copy-start.6 = (f32[1,64,1024]{2,1,0:T(8,128)S(1)}, f32[1,64,1024]{2,1,0:T(8,128)}, u32[]{:S(2)}) copy-start(f32[1,64,1024]{2,1,0:T(8,128)} %param.11) | copy-start | bytes 786436
Sparse Core Ops, SparseCore 0:
  10.3 29.8 reduce-scatter.4
  42.6 29.8 reduce-scatter.2
where the time goes:
time: 160 us; the launch traced here: 158 us
  blocking collectives  70.3 us (44%)
  waiting for transfers between devices  63.6 us (40%)
  between operations  16.2 us (10%)
  other arithmetic  6.45 us (4%)
  local copies, waits for them, and re-layouts  1.67 us (1%)
    psum x1, blocking collectives, body(): squares = lax.psum(partial_value, ('group', 'shard'))  39 us
    reduce_scatter x1, waiting for transfers between devices, body(): lax.psum_scatter(exit_local, 'group', scatter_dimension=0, tiled=True)  31.5 us
    reduce_scatter x1, waiting for transfers between devices, body(): lax.psum_scatter(entry_local, 'group', scatter_dimension=0, tiled=True)  30.7 us
    all_gather x1, blocking collectives, body(): entry_weights = lax.all_gather(entry_round, 'group', axis=0, tiled=True)  16.4 us
    all_gather x1, blocking collectives, body(): exit_weights = lax.all_gather(exit_round, 'group', axis=0, tiled=True)  14.9 us
  transfers between devices with their start and end apart: 2, of which 2 were waited for; matrix products, arithmetic and copies ran while one was open for 1% of the time, Pallas kernels for 0%

commit v1 on v0

v1 whole, which is shorter than its diff:
```python
import functools

import jax
import jax.numpy as jnp
from jax import lax
from jax.experimental import pallas as pl
from jax.experimental.pallas import tpu as pltpu
from jax.sharding import PartitionSpec as P

beta_first = 0.9
beta_second = 0.95
learn_rate = 0.01
decay_rate = 0.1
epsilon = 1e-08
correct_first = 1.0 - 0.9**40
correct_second = 1.0 - 0.95**40

MESH = pl.DeviceIdType.MESH


def adamw_step(params, mean, square, total, clip):
    grads = clip * total
    moment = beta_first * mean + (1.0 - beta_first) * grads
    variance = beta_second * square + (1.0 - beta_second) * grads * grads
    update = moment / correct_first / (jnp.sqrt(variance / correct_second) + epsilon)
    master = params - learn_rate * (update + decay_rate * params)
    return (master, moment, variance)


def squares_tile(total):
    rows, width = total.shape
    squared = total * total
    folded = squared[0:8]
    for row in range(8, rows, 8):
        folded = folded + squared[row : row + 8]
    tile = folded[:, 0:128]
    for column in range(128, width, 128):
        tile = tile + folded[:, column : column + 128]
    return tile


def kernel(
    groups,
    shards,
    count,
    pieces,
    entry_grads, exit_grads,
    entry_params, exit_params, entry_mean, exit_mean, entry_square, exit_square,
    entry_master, exit_master, entry_moment, exit_moment,
    entry_variance, exit_variance, entry_weights, exit_weights,
    entry_x, exit_x, entry_held, exit_held,
    entry_p, exit_p, entry_m, exit_m, entry_v, exit_v, entry_w, exit_w,
    group_tiles, shard_tiles,
    load_sem, state_sem, store_sem,
    sum_send, sum_recv, tile_send, tile_recv, shard_send, shard_recv,
    gather_send, gather_recv,
):
    me = lax.axis_index("group")
    shard = lax.axis_index("shard")
    kinds = 2
    grads = (entry_grads, exit_grads)
    x = (entry_x, exit_x)
    held = (entry_held, exit_held)
    states = ((entry_p, entry_m, entry_v), (exit_p, exit_m, exit_v))
    state_in = (
        (entry_params, entry_mean, entry_square),
        (exit_params, exit_mean, exit_square),
    )
    state_out = (
        (entry_master, entry_moment, entry_variance),
        (exit_master, exit_moment, exit_variance),
    )
    own_w = (entry_w, exit_w)
    weights = (entry_weights, exit_weights)
    rows = entry_p.shape[0]
    steps = groups - 1

    loads = [pltpu.make_async_copy(grads[k], x[k], load_sem.at[k]) for k in range(kinds)]
    state_loads = [
        pltpu.make_async_copy(state_in[k][i], states[k][i], state_sem.at[k, i])
        for k in range(kinds)
        for i in range(3)
    ]
    for copy in loads + state_loads:
        copy.start()

    barrier = pltpu.get_barrier_semaphore()
    for offset in range(1, groups):
        pl.semaphore_signal(
            barrier, inc=1, device_id={"group": lax.rem(me + offset, groups)}, device_id_type=MESH
        )
    for offset in range(1, shards):
        pl.semaphore_signal(
            barrier, inc=1, device_id={"shard": lax.rem(shard + offset, shards)}, device_id_type=MESH
        )
    pl.semaphore_wait(barrier, groups - 1 + shards - 1)
    for copy in loads:
        copy.wait()

    def row_block(index):
        return pl.ds(pl.multiple_of(index * rows, rows), rows)

    def place_in(stream):
        return me + stream * (groups - 1 - 2 * me)

    def peer_in(stream):
        return {"group": me + 1 - 2 * stream}

    def wanted(stream, step):
        return (groups - 1 - step) * (1 - stream) + step * stream

    def sum_copy(stream, step, k, source):
        return pltpu.make_async_remote_copy(
            src_ref=source,
            dst_ref=held[k].at[stream, step],
            send_sem=sum_send.at[stream, step, k],
            recv_sem=sum_recv.at[stream, step, k],
            device_id=peer_in(stream),
            device_id_type=MESH,
        )

    near = lax.select(me < groups // 2, 0, 1)

    @pl.when((me == 0) | (me == groups - 1))
    def _():
        order = [(step, k) for step in range(steps) for k in range(kinds)]
        copies = [
            sum_copy(near, step, k, x[k].at[row_block(wanted(near, step))]) for step, k in order
        ]
        for i, copy in enumerate(copies):
            if i >= 2:
                copies[i - 2].wait_send()
            copy.start()
        for copy in copies[-2:]:
            copy.wait_send()

    own = row_block(me)
    for step in range(steps):
        target = groups - 1 - step
        for stream in (near, 1 - near):
            place = place_in(stream)
            for k in range(kinds):

                @pl.when((place > 0) & (place <= target))
                def _(stream=stream, place=place, k=k):
                    slot = held[k].at[stream, step]
                    copy = sum_copy(stream, step, k, slot)
                    copy.wait_recv()

                    @pl.when(place < target)
                    def _():
                        slot[...] += x[k][row_block(wanted(stream, step))]
                        copy.start()

                    @pl.when(place == target)
                    def _():
                        x[k][own] += slot[...]

    group_tiles[me] = squares_tile(x[0][own]) + squares_tile(x[1][own])
    tile_copies = [
        pltpu.make_async_remote_copy(
            src_ref=group_tiles.at[me],
            dst_ref=group_tiles.at[me],
            send_sem=tile_send.at[offset],
            recv_sem=tile_recv.at[offset],
            device_id={"group": lax.rem(me + offset, groups)},
            device_id_type=MESH,
        )
        for offset in range(1, groups)
    ]
    for copy in tile_copies:
        copy.start()
    for copy in state_loads:
        copy.wait()
    for copy in tile_copies:
        copy.wait_recv()
    shard_tiles[shard] = jnp.sum(group_tiles[...], axis=0)
    shard_copies = [
        pltpu.make_async_remote_copy(
            src_ref=shard_tiles.at[shard],
            dst_ref=shard_tiles.at[shard],
            send_sem=shard_send.at[offset],
            recv_sem=shard_recv.at[offset],
            device_id={"shard": lax.rem(shard + offset, shards)},
            device_id_type=MESH,
        )
        for offset in range(1, shards)
    ]
    for copy in shard_copies:
        copy.start()
    for copy in shard_copies:
        copy.wait_recv()
    squares = jnp.sum(jnp.sum(shard_tiles[...], axis=0), keepdims=True)
    limit = jnp.sqrt(jnp.full((1, 1), count, jnp.float32))
    clip = jnp.minimum(jnp.float32(1.0), limit / (jnp.sqrt(squares) + 1e-06))

    height = rows // pieces

    def gather_copy(stream, distance, chunk, source_group, source=None):
        k, piece = chunk // pieces, chunk % pieces
        place = pl.ds(pl.multiple_of(source_group * rows + piece * height, height), height)
        return pltpu.make_async_remote_copy(
            src_ref=weights[k].at[place] if source is None else source,
            dst_ref=weights[k].at[place],
            send_sem=gather_send.at[stream, distance, chunk],
            recv_sem=gather_recv.at[stream, distance, chunk],
            device_id=peer_in(stream),
            device_id_type=MESH,
        )

    def has_next(stream):
        return me < groups - 1 if stream == 0 else me > 0

    chunks = kinds * pieces
    stores = []
    for chunk in range(chunks):
        k, piece = chunk // pieces, chunk % pieces
        part = slice(piece * height, (piece + 1) * height)
        p, m, v = states[k]
        at = pl.ds(pl.multiple_of(me * rows + piece * height, height), height)
        master, moment, variance = adamw_step(p[part], m[part], v[part], x[k][at], clip)
        own_w[k][part] = master.astype(jnp.bfloat16)
        source = own_w[k].at[part]
        for stream in range(2):

            @pl.when(has_next(stream))
            def _(stream=stream):
                gather_copy(stream, 0, chunk, me, source).start()

        p[part], m[part], v[part] = master, moment, variance
        copies = [pltpu.make_async_copy(source, weights[k].at[at], store_sem.at[chunk, 3])]
        for i in range(3):
            copies.append(
                pltpu.make_async_copy(
                    states[k][i].at[part], state_out[k][i].at[part], store_sem.at[chunk, i]
                )
            )
        for copy in copies:
            copy.start()
        stores += copies

    for distance in range(1, groups):
        for chunk in range(chunks):
            for stream in range(2):
                origin = me - distance if stream == 0 else me + distance

                @pl.when(origin >= 0 if stream == 0 else origin < groups)
                def _(stream=stream, origin=origin):
                    gather_copy(stream, distance - 1, chunk, origin).wait_recv()

                    @pl.when(has_next(stream))
                    def _():
                        gather_copy(stream, distance, chunk, origin).start()

    for distance in range(groups - 1):
        for chunk in range(chunks):
            for stream in range(2):
                origin = me - distance if stream == 0 else me + distance

                @pl.when(
                    has_next(stream) & (origin >= 0 if stream == 0 else origin < groups)
                )
                def _(stream=stream, origin=origin):
                    gather_copy(stream, distance, chunk, origin).wait_send()

    for step in range(steps):
        target = groups - 1 - step
        for stream in (near, 1 - near):
            place = place_in(stream)
            for k in range(kinds):

                @pl.when((place > 0) & (place < target))
                def _(stream=stream, k=k):
                    sum_copy(stream, step, k, held[k].at[stream, step]).wait_send()

    for copy in tile_copies + shard_copies:
        copy.wait_send()
    for copy in stores:
        copy.wait()


def body(groups, shards, *args):
    entry_grads, exit_grads, *state = args
    full, entry_width = entry_grads.shape[2:]
    exit_width = exit_grads.shape[3]
    rows = full // groups
    pieces = max(1, rows // 32)
    count = full * (entry_width + exit_width) * shards
    widths = (entry_width, exit_width)
    f32, bf16 = jnp.float32, jnp.bfloat16
    operands = [entry_grads.reshape(full, entry_width), exit_grads.reshape(full, exit_width)]
    operands += [a.reshape(a.shape[1:]) for a in state]
    small = [jax.ShapeDtypeStruct((rows, w), f32) for w in widths]
    out_shape = small * 3 + [jax.ShapeDtypeStruct((full, w), bf16) for w in widths]
    chunks = 2 * pieces
    dma = pltpu.SemaphoreType.DMA
    scratch = (
        [pltpu.VMEM((full, w), f32) for w in widths]
        + [pltpu.VMEM((2, groups - 1, rows, w), f32) for w in widths]
        + [pltpu.VMEM((rows, w), f32) for w in widths] * 3
        + [pltpu.VMEM((rows, w), bf16) for w in widths]
        + [pltpu.VMEM((groups, 8, 128), f32), pltpu.VMEM((shards, 8, 128), f32)]
        + [dma((2,)), dma((2, 3)), dma((chunks, 4))]
        + [dma((2, groups - 1, 2))] * 2
        + [dma((groups,))] * 2
        + [dma((shards,))] * 2
        + [dma((2, groups, chunks))] * 2
    )
    outs = pl.pallas_call(
        functools.partial(kernel, groups, shards, float(count), pieces),
        out_shape=out_shape,
        in_specs=[pl.BlockSpec(memory_space=pl.ANY)] * 8,
        out_specs=[pl.BlockSpec(memory_space=pl.ANY)] * 8,
        scratch_shapes=scratch,
        compiler_params=pltpu.CompilerParams(
            collective_id=0, has_side_effects=True, vmem_limit_bytes=48 * 1024 * 1024
        ),
    )(*operands)
    return tuple(a[None] for a in outs)


def solution(mesh):
    grads = P("group", "shard", None, None)
    state = P("shard", "group", None)
    gathered = P("shard", None, None)
    return jax.shard_map(
        functools.partial(body, mesh.shape["group"], mesh.shape["shard"]),
        mesh=mesh,
        in_specs=(grads,) * 2 + (state,) * 6,
        out_specs=(state,) * 6 + (gathered,) * 2,
        check_vma=False,
    )
```

time: 160 us -> 87.4 us (0.55)
  Pallas kernels: 0 us -> 73.5 us
  blocking collectives: 70.3 us -> 0 us
  waiting for transfers between devices: 63.6 us -> 0 us
  between operations: 16.2 us -> 0.66 us
  local copies, waits for them, and re-layouts: 1.67 us -> 12.9 us
  other arithmetic: 6.45 us -> 0 us
    pallas_call x0 -> x1, Pallas kernels: none -> 73.5 us  [body(): pl.pallas_call(functools.partial(kernel, groups, shards, float(count), pi...]
    reduce_scatter x2 -> x0, waiting for transfers between devices: 62.2 us -> none  [the longest x1 31.5 us: body(): lax.psum_scatter(exit_local, 'group', scatter_dimension=0, tiled=True)]
    psum x1 -> x0, blocking collectives: 39 us -> none  [body(): squares = lax.psum(partial_value, ('group', 'shard'))]
    all_gather x2 -> x0, blocking collectives: 31.3 us -> none  [the longest x1 16.4 us: body(): entry_weights = lax.all_gather(entry_round, 'group', axis=0, tiled=True)]
    unnamed x16 -> x22, local copies, waits for them, and re-layouts: 1.67 us -> 12.9 us
    reduce_sum x2 -> x0, other arithmetic: 3.28 us -> none  [the longest x1 1.66 us: body(): jnp.sum(entry_total * entry_total) + jnp.sum(exit_total * exit_total)]
    convert_element_type x2 -> x0, other arithmetic: 3.17 us -> none  [the longest x1 2.16 us: body(): entry_round = entry_master.astype(jnp.bfloat16)]
  transfers between devices with their start and end apart: 2 -> 0, of which waited for: 2 -> 0; matrix products, arithmetic and copies ran while one was open for 1% -> 0% of each run, Pallas kernels for 0% -> 0%
where the time goes in v1:
time: 87.4 us; the launch traced here: 87 us
  Pallas kernels  73.5 us (84%)
  local copies, waits for them, and re-layouts  12.9 us (15%)
    pallas_call x1, Pallas kernels, body(): pl.pallas_call(functools.partial(kernel, groups, shards, float(count), pi...  73.5 us
    unnamed x22, local copies, waits for them, and re-layouts  12.9 us

profile of v1, /device:TPU:0, one launch (start us, length us, event | category | flops | bytes accessed | tf_op | source)
XLA Modules:
  0.0 87.0 jit_solution(14624461036249759068)
XLA Ops:
  0.6 0.0 copy-start
  0.6 1.2 %copy-done = f32[1,1,256,1024]{3,2,1,0:T(8,128)S(1)} copy-done((f32[1,1,256,1024]{3,2,1,0:T(8,128)S(1)}, f32[1,1,256,1024]{3,2,1,0:T(8,128)}, u32[]{:S(2)}) %copy-start) | copy-done | bytes 1048600
  1.9 0.0 copy-start.1
  1.9 1.0 %copy-done.1 = f32[1,64,1280]{2,1,0:T(8,128)S(1)} copy-done((f32[1,64,1280]{2,1,0:T(8,128)S(1)}, f32[1,64,1280]{2,1,0:T(8,128)}, u32[]{:S(2)}) %copy-start.1) | copy-done | bytes 327704
  2.8 0.0 copy-start.2
  2.8 1.0 %copy-done.2 = f32[1,64,1280]{2,1,0:T(8,128)S(1)} copy-done((f32[1,64,1280]{2,1,0:T(8,128)S(1)}, f32[1,64,1280]{2,1,0:T(8,128)}, u32[]{:S(2)}) %copy-start.2) | copy-done | bytes 327704
  3.8 0.0 copy-start.3
  3.8 1.0 %copy-done.3 = f32[1,64,1280]{2,1,0:T(8,128)S(1)} copy-done((f32[1,64,1280]{2,1,0:T(8,128)S(1)}, f32[1,64,1280]{2,1,0:T(8,128)}, u32[]{:S(2)}) %copy-start.3) | copy-done | bytes 327704
  4.8 0.0 copy-start.4
  4.8 0.9 %copy-done.4 = f32[1,64,1024]{2,1,0:T(8,128)S(1)} copy-done((f32[1,64,1024]{2,1,0:T(8,128)S(1)}, f32[1,64,1024]{2,1,0:T(8,128)}, u32[]{:S(2)}) %copy-start.4) | copy-done | bytes 262168
  5.7 0.0 copy-start.5
  5.7 0.9 %copy-done.5 = f32[1,64,1024]{2,1,0:T(8,128)S(1)} copy-done((f32[1,64,1024]{2,1,0:T(8,128)S(1)}, f32[1,64,1024]{2,1,0:T(8,128)}, u32[]{:S(2)}) %copy-start.5) | copy-done | bytes 262168
  6.7 0.0 copy-start.6
  6.7 0.9 %copy-done.6 = f32[1,64,1024]{2,1,0:T(8,128)S(1)} copy-done((f32[1,64,1024]{2,1,0:T(8,128)S(1)}, f32[1,64,1024]{2,1,0:T(8,128)}, u32[]{:S(2)}) %copy-start.6) | copy-done | bytes 262168
  7.6 73.5 %shard_map.143 = (f32[64,1280]{1,0:T(8,128)S(1)}, f32[64,1024]{1,0:T(8,128)S(1)}, f32[64,1280]{1,0:T(8,128)S(1)}, f32[64,1024]{1,0:T(8,128)S(1)}, f32[64,1280]{1...) custom-call(f32[256,1280]{1,0:T(8,128)} %bitcast.31, ...), custom_call_target="tpu_custom_call" | custom-call | tf_op jit(solution)/shard_map/pallas_call | solution.py:309
  81.1 0.7 copy.24
  81.8 0.7 copy.25
  82.5 0.7 copy.26
  83.3 0.7 copy.27
  84.0 0.7 copy.28
  84.7 0.7 copy.29
  85.4 0.8 copy.30
  86.2 0.8 copy.31
Async XLA Ops:
  0.6 1.2 %copy-start = (f32[1,1,256,1024]{3,2,1,0:T(8,128)S(1)}, f32[1,1,256,1024]{3,2,1,0:T(8,128)}, u32[]{:S(2)}) copy-start(f32[1,1,256,1024]{3,2,1,0:T(8,128)} %param.9) | copy-start | bytes 3145732
  1.9 1.0 %copy-start.1 = (f32[1,64,1280]{2,1,0:T(8,128)S(1)}, f32[1,64,1280]{2,1,0:T(8,128)}, u32[]{:S(2)}) copy-start(f32[1,64,1280]{2,1,0:T(8,128)} %param.10) | copy-start | bytes 983044
  2.8 1.0 %copy-start.2 = (f32[1,64,1280]{2,1,0:T(8,128)S(1)}, f32[1,64,1280]{2,1,0:T(8,128)}, u32[]{:S(2)}) copy-start(f32[1,64,1280]{2,1,0:T(8,128)} %param.12) | copy-start | bytes 983044
  3.8 1.0 %copy-start.3 = (f32[1,64,1280]{2,1,0:T(8,128)S(1)}, f32[1,64,1280]{2,1,0:T(8,128)}, u32[]{:S(2)}) copy-start(f32[1,64,1280]{2,1,0:T(8,128)} %param.14) | copy-start | bytes 983044
  4.8 0.9 %copy-start.4 = (f32[1,64,1024]{2,1,0:T(8,128)S(1)}, f32[1,64,1024]{2,1,0:T(8,128)}, u32[]{:S(2)}) copy-start(f32[1,64,1024]{2,1,0:T(8,128)} %param.11) | copy-start | bytes 786436
  5.7 0.9 %copy-start.5 = (f32[1,64,1024]{2,1,0:T(8,128)S(1)}, f32[1,64,1024]{2,1,0:T(8,128)}, u32[]{:S(2)}) copy-start(f32[1,64,1024]{2,1,0:T(8,128)} %param.13) | copy-start | bytes 786436
  6.7 0.9 %copy-start.6 = (f32[1,64,1024]{2,1,0:T(8,128)S(1)}, f32[1,64,1024]{2,1,0:T(8,128)}, u32[]{:S(2)}) copy-start(f32[1,64,1024]{2,1,0:T(8,128)} %param.15) | copy-start | bytes 786436

commit v2 on v1

--- a/solution.py
+++ b/solution.py
@@ -279,6 +279,31 @@
         copy.wait()
 
 
+def copy_kernel(*refs):
+    count = len(refs) // 2
+    sem = refs[-1]
+    copies = [
+        pltpu.make_async_copy(refs[i], refs[count + i], sem.at[i]) for i in range(count)
+    ]
+    for copy in copies:
+        copy.start()
+    for copy in copies:
+        copy.wait()
+
+
+def copy_out(arrays):
+    moved = sum(2 * a.size * a.dtype.itemsize for a in arrays)
+    return pl.pallas_call(
+        copy_kernel,
+        out_shape=[jax.ShapeDtypeStruct(a.shape, a.dtype) for a in arrays],
+        in_specs=[pl.BlockSpec(memory_space=pltpu.HBM)] * len(arrays),
+        out_specs=[pl.BlockSpec(memory_space=pltpu.HBM)] * len(arrays),
+        scratch_shapes=[pltpu.SemaphoreType.DMA((len(arrays),))],
+        cost_estimate=pl.CostEstimate(flops=0, bytes_accessed=moved, transcendentals=0),
+        compiler_params=pltpu.CompilerParams(vmem_limit_bytes=64 * 1024 * 1024),
+    )(*arrays)
+
+
 def body(groups, shards, *args):
     entry_grads, exit_grads, *state = args
     full, entry_width = entry_grads.shape[2:]
@@ -309,14 +334,14 @@
     outs = pl.pallas_call(
         functools.partial(kernel, groups, shards, float(count), pieces),
         out_shape=out_shape,
-        in_specs=[pl.BlockSpec(memory_space=pl.ANY)] * 8,
-        out_specs=[pl.BlockSpec(memory_space=pl.ANY)] * 8,
+        in_specs=[pl.BlockSpec(memory_space=pltpu.HBM)] * 8,
+        out_specs=[pl.BlockSpec(memory_space=pltpu.HBM)] * 8,
         scratch_shapes=scratch,
         compiler_params=pltpu.CompilerParams(
-            collective_id=0, has_side_effects=True, vmem_limit_bytes=48 * 1024 * 1024
+            collective_id=0, has_side_effects=True, vmem_limit_bytes=64 * 1024 * 1024
         ),
     )(*operands)
-    return tuple(a[None] for a in outs)
+    return tuple(a[None] for a in copy_out(outs))
 
 
 def solution(mesh):

time: 87.4 us -> 166 us (1.90)
  Pallas kernels: 73.5 us -> 165 us
  local copies, waits for them, and re-layouts: 12.9 us -> 0 us
    pallas_call x0 -> x1, Pallas kernels: none -> 90.5 us  [copy_out(): pl.pallas_call(copy_kernel, out_shape=[jax.ShapeDtypeStruct(a.shape, a.dt...]
    unnamed x22 -> x0, local copies, waits for them, and re-layouts: 12.9 us -> none
where the time goes in v2:
time: 166 us; the launch traced here: 165 us
  Pallas kernels  165 us (99%)
    pallas_call x1, Pallas kernels, copy_out(): pl.pallas_call(copy_kernel, out_shape=[jax.ShapeDtypeStruct(a.shape, a.dt...  90.5 us
    pallas_call x1, Pallas kernels, body(): pl.pallas_call(functools.partial(kernel, groups, shards, float(count), pi...  74.3 us

profile of v2, /device:TPU:0, one launch (start us, length us, event | category | flops | bytes accessed | tf_op | source)
XLA Modules:
  0.0 165.5 jit_solution(6280323194858922082)
XLA Ops:
  0.6 74.3 %shard_map.143 = (f32[64,1280]{1,0:T(8,128)}, f32[64,1024]{1,0:T(8,128)}, f32[64,1280]{1,0:T(8,128)}, f32[64,1024]{1,0:T(8,128)}, f32[64,1280]{1,0:T(8,128)}, /*...) custom-call(f32[256,1280]{1,0:T(8,128)} %bitcast.16, f32[256,1024]{1,0:T(8,128)} %bitcast.17, ...), custom_call_target="tpu_custom_call" | custom-call | tf_op jit(solution)/shard_map/pallas_call | solution.py:334
  75.0 90.5 %shard_map.144 = (f32[64,1280]{1,0:T(8,128)}, f32[64,1024]{1,0:T(8,128)}, f32[64,1280]{1,0:T(8,128)}, f32[64,1024]{1,0:T(8,128)}, f32[64,1280]{1,0:T(8,128)}, /*...) custom-call(f32[64,1280]{1,0:T(8,128)} %get-tuple-element.24.refs_0_, ...), custom_call_target="tpu_custom_call" | custom-call | bytes 5898240 | tf_op jit(solution)/shard_map/pallas_call | solution.py:296

commit v3 on v2

--- a/solution.py
+++ b/solution.py
@@ -51,7 +51,7 @@
     entry_x, exit_x, entry_held, exit_held,
     entry_p, exit_p, entry_m, exit_m, entry_v, exit_v, entry_w, exit_w,
     group_tiles, shard_tiles,
-    load_sem, state_sem, store_sem,
+    load_sem, state_sem, store_sem, weight_sem,
     sum_send, sum_recv, tile_send, tile_recv, shard_send, shard_recv,
     gather_send, gather_recv,
 ):
@@ -70,7 +70,7 @@
         (entry_master, entry_moment, entry_variance),
         (exit_master, exit_moment, exit_variance),
     )
-    own_w = (entry_w, exit_w)
+    gathered = (entry_w, exit_w)
     weights = (entry_weights, exit_weights)
     rows = entry_p.shape[0]
     steps = groups - 1
@@ -196,16 +196,26 @@
 
     height = rows // pieces
 
-    def gather_copy(stream, distance, chunk, source_group, source=None):
+    def piece_of(source_group, piece):
+        return pl.ds(pl.multiple_of(source_group * rows + piece * height, height), height)
+
+    def gather_copy(stream, distance, chunk, source_group):
         k, piece = chunk // pieces, chunk % pieces
-        place = pl.ds(pl.multiple_of(source_group * rows + piece * height, height), height)
+        block = gathered[k].at[piece_of(source_group, piece)]
         return pltpu.make_async_remote_copy(
-            src_ref=weights[k].at[place] if source is None else source,
-            dst_ref=weights[k].at[place],
+            src_ref=block,
+            dst_ref=block,
             send_sem=gather_send.at[stream, distance, chunk],
             recv_sem=gather_recv.at[stream, distance, chunk],
             device_id=peer_in(stream),
             device_id_type=MESH,
+        )
+
+    def weight_store(stream, distance, chunk, source_group):
+        k, piece = chunk // pieces, chunk % pieces
+        place = piece_of(source_group, piece)
+        return pltpu.make_async_copy(
+            gathered[k].at[place], weights[k].at[place], weight_sem.at[stream, distance, chunk]
         )
 
     def has_next(stream):
@@ -217,18 +227,17 @@
         k, piece = chunk // pieces, chunk % pieces
         part = slice(piece * height, (piece + 1) * height)
         p, m, v = states[k]
-        at = pl.ds(pl.multiple_of(me * rows + piece * height, height), height)
+        at = piece_of(me, piece)
         master, moment, variance = adamw_step(p[part], m[part], v[part], x[k][at], clip)
-        own_w[k][part] = master.astype(jnp.bfloat16)
-        source = own_w[k].at[part]
+        gathered[k][at] = master.astype(jnp.bfloat16)
         for stream in range(2):
 
             @pl.when(has_next(stream))
             def _(stream=stream):
-                gather_copy(stream, 0, chunk, me, source).start()
+                gather_copy(stream, 0, chunk, me).start()
 
         p[part], m[part], v[part] = master, moment, variance
-        copies = [pltpu.make_async_copy(source, weights[k].at[at], store_sem.at[chunk, 3])]
+        copies = [weight_store(0, 0, chunk, me)]
         for i in range(3):
             copies.append(
                 pltpu.make_async_copy(
@@ -252,6 +261,8 @@
                     def _():
                         gather_copy(stream, distance, chunk, origin).start()
 
+                    weight_store(stream, distance, chunk, origin).start()
+
     for distance in range(groups - 1):
         for chunk in range(chunks):
             for stream in range(2):
@@ -263,6 +274,15 @@
                 def _(stream=stream, origin=origin):
                     gather_copy(stream, distance, chunk, origin).wait_send()
 
+    for distance in range(1, groups):
+        for chunk in range(chunks):
+            for stream in range(2):
+                origin = me - distance if stream == 0 else me + distance
+
+                @pl.when(origin >= 0 if stream == 0 else origin < groups)
+                def _(stream=stream, origin=origin):
+                    weight_store(stream, distance, chunk, origin).wait()
+
     for step in range(steps):
         target = groups - 1 - step
         for stream in (near, 1 - near):
@@ -280,14 +300,17 @@
 
 
 def copy_kernel(*refs):
-    count = len(refs) // 2
-    sem = refs[-1]
-    copies = [
-        pltpu.make_async_copy(refs[i], refs[count + i], sem.at[i]) for i in range(count)
-    ]
-    for copy in copies:
+    count = (len(refs) - 2) // 3
+    ins, outs, held = refs[:count], refs[count : 2 * count], refs[2 * count : 3 * count]
+    load_sem, store_sem = refs[-2:]
+    loads = [pltpu.make_async_copy(ins[i], held[i], load_sem.at[i]) for i in range(count)]
+    stores = [pltpu.make_async_copy(held[i], outs[i], store_sem.at[i]) for i in range(count)]
+    for copy in loads:
         copy.start()
-    for copy in copies:
+    for load, store in zip(loads, stores):
+        load.wait()
+        store.start()
+    for copy in stores:
         copy.wait()
 
 
@@ -298,7 +321,8 @@
         out_shape=[jax.ShapeDtypeStruct(a.shape, a.dtype) for a in arrays],
         in_specs=[pl.BlockSpec(memory_space=pltpu.HBM)] * len(arrays),
         out_specs=[pl.BlockSpec(memory_space=pltpu.HBM)] * len(arrays),
-        scratch_shapes=[pltpu.SemaphoreType.DMA((len(arrays),))],
+        scratch_shapes=[pltpu.VMEM(a.shape, a.dtype) for a in arrays]
+        + [pltpu.SemaphoreType.DMA((len(arrays),))] * 2,
         cost_estimate=pl.CostEstimate(flops=0, bytes_accessed=moved, transcendentals=0),
         compiler_params=pltpu.CompilerParams(vmem_limit_bytes=64 * 1024 * 1024),
     )(*arrays)
@@ -323,9 +347,9 @@
         [pltpu.VMEM((full, w), f32) for w in widths]
         + [pltpu.VMEM((2, groups - 1, rows, w), f32) for w in widths]
         + [pltpu.VMEM((rows, w), f32) for w in widths] * 3
-        + [pltpu.VMEM((rows, w), bf16) for w in widths]
+        + [pltpu.VMEM((full, w), bf16) for w in widths]
         + [pltpu.VMEM((groups, 8, 128), f32), pltpu.VMEM((shards, 8, 128), f32)]
-        + [dma((2,)), dma((2, 3)), dma((chunks, 4))]
+        + [dma((2,)), dma((2, 3)), dma((chunks, 3)), dma((2, groups, chunks))]
         + [dma((2, groups - 1, 2))] * 2
         + [dma((groups,))] * 2
         + [dma((shards,))] * 2

time: 166 us -> 78.7 us (0.47)
  Pallas kernels: 165 us -> 77.9 us
    pallas_call x1, Pallas kernels: 90.5 us -> 2.78 us  [copy_out(): pl.pallas_call(copy_kernel, out_shape=[jax.ShapeDtypeStruct(a.shape, a.dt...]
where the time goes in v3:
time: 78.7 us; the launch traced here: 78.5 us
  Pallas kernels  77.9 us (99%)
    pallas_call x1, Pallas kernels, body(): pl.pallas_call(functools.partial(kernel, groups, shards, float(count), pi...  75.1 us
    pallas_call x1, Pallas kernels, copy_out(): pl.pallas_call(copy_kernel, out_shape=[jax.ShapeDtypeStruct(a.shape, a.dt...  2.78 us

profile of v3, /device:TPU:0, one launch (start us, length us, event | category | flops | bytes accessed | tf_op | source)
XLA Modules:
  0.0 78.5 jit_solution(2786683689706715754)
XLA Ops:
  0.6 75.1 %shard_map.143 = (f32[64,1280]{1,0:T(8,128)}, f32[64,1024]{1,0:T(8,128)}, f32[64,1280]{1,0:T(8,128)}, f32[64,1024]{1,0:T(8,128)}, f32[64,1280]{1,0:T(8,128)}, /*...) custom-call(f32[256,1280]{1,0:T(8,128)} %bitcast.16, f32[256,1024]{1,0:T(8,128)} %bitcast.17, ...), custom_call_target="tpu_custom_call" | custom-call | tf_op jit(solution)/shard_map/pallas_call | solution.py:358
  75.7 2.8 %shard_map.144 = (f32[64,1280]{1,0:T(8,128)}, f32[64,1024]{1,0:T(8,128)}, f32[64,1280]{1,0:T(8,128)}, f32[64,1024]{1,0:T(8,128)}, f32[64,1280]{1,0:T(8,128)}, /*...) custom-call(f32[64,1280]{1,0:T(8,128)} %get-tuple-element.24.refs_0_, ...), custom_call_target="tpu_custom_call" | custom-call | bytes 5898240 | tf_op jit(solution)/shard_map/pallas_call | solution.py:319

commit v4 on v3

--- a/solution.py
+++ b/solution.py
@@ -75,30 +75,42 @@
     rows = entry_p.shape[0]
     steps = groups - 1
 
-    loads = [pltpu.make_async_copy(grads[k], x[k], load_sem.at[k]) for k in range(kinds)]
+    def row_block(index):
+        return pl.ds(pl.multiple_of(index * rows, rows), rows)
+
+    near = lax.select(me < groups // 2, 0, 1)
+
+    def wanted(stream, step):
+        return (groups - 1 - step) * (1 - stream) + step * stream
+
+    def load(k, step):
+        block = row_block(wanted(near, step))
+        return pltpu.make_async_copy(grads[k].at[block], x[k].at[block], load_sem.at[step, k])
+
+    for step in range(groups):
+        for k in range(kinds):
+            load(k, step).start()
+
+    barrier = pltpu.get_barrier_semaphore()
+    for offset in range(1, groups):
+        pl.semaphore_signal(
+            barrier, inc=1, device_id={"group": lax.rem(me + offset, groups)}, device_id_type=MESH
+        )
+    for offset in range(1, shards):
+        pl.semaphore_signal(
+            barrier, inc=1, device_id={"shard": lax.rem(shard + offset, shards)}, device_id_type=MESH
+        )
+    pl.semaphore_wait(barrier, groups - 1 + shards - 1)
     state_loads = [
         pltpu.make_async_copy(state_in[k][i], states[k][i], state_sem.at[k, i])
         for k in range(kinds)
         for i in range(3)
     ]
-    for copy in loads + state_loads:
+    for copy in state_loads:
         copy.start()
 
-    barrier = pltpu.get_barrier_semaphore()
-    for offset in range(1, groups):
-        pl.semaphore_signal(
-            barrier, inc=1, device_id={"group": lax.rem(me + offset, groups)}, device_id_type=MESH
-        )
-    for offset in range(1, shards):
-        pl.semaphore_signal(
-            barrier, inc=1, device_id={"shard": lax.rem(shard + offset, shards)}, device_id_type=MESH
-        )
-    pl.semaphore_wait(barrier, groups - 1 + shards - 1)
-    for copy in loads:
-        copy.wait()
-
-    def row_block(index):
-        return pl.ds(pl.multiple_of(index * rows, rows), rows)
+    height = rows // pieces
+    chunks = kinds * pieces
 
     def place_in(stream):
         return me + stream * (groups - 1 - 2 * me)
@@ -106,55 +118,70 @@
     def peer_in(stream):
         return {"group": me + 1 - 2 * stream}
 
-    def wanted(stream, step):
-        return (groups - 1 - step) * (1 - stream) + step * stream
-
-    def sum_copy(stream, step, k, source):
+    def piece_of(block, piece):
+        return pl.ds(pl.multiple_of(block * rows + piece * height, height), height)
+
+    def slot_of(stream, step, chunk):
+        k, piece = chunk // pieces, chunk % pieces
+        return held[k].at[stream, step, slice(piece * height, (piece + 1) * height)]
+
+    def sum_copy(stream, step, chunk, source):
         return pltpu.make_async_remote_copy(
             src_ref=source,
-            dst_ref=held[k].at[stream, step],
-            send_sem=sum_send.at[stream, step, k],
-            recv_sem=sum_recv.at[stream, step, k],
+            dst_ref=slot_of(stream, step, chunk),
+            send_sem=sum_send.at[stream, step, chunk],
+            recv_sem=sum_recv.at[stream, step, chunk],
             device_id=peer_in(stream),
             device_id_type=MESH,
         )
 
-    near = lax.select(me < groups // 2, 0, 1)
-
     @pl.when((me == 0) | (me == groups - 1))
     def _():
-        order = [(step, k) for step in range(steps) for k in range(kinds)]
-        copies = [
-            sum_copy(near, step, k, x[k].at[row_block(wanted(near, step))]) for step, k in order
-        ]
-        for i, copy in enumerate(copies):
-            if i >= 2:
-                copies[i - 2].wait_send()
-            copy.start()
+        copies = []
+        for step in range(steps):
+            for chunk in range(chunks):
+                k, piece = chunk // pieces, chunk % pieces
+                if piece == 0:
+                    load(k, step).wait()
+                source = x[k].at[piece_of(wanted(near, step), piece)]
+                copies.append(sum_copy(near, step, chunk, source))
+                if len(copies) > 2:
+                    copies[-3].wait_send()
+                copies[-1].start()
         for copy in copies[-2:]:
             copy.wait_send()
+
+    @pl.when((me > 0) & (me < groups - 1))
+    def _():
+        for step in range(steps):
+            for k in range(kinds):
+                load(k, step).wait()
+
+    for k in range(kinds):
+        load(k, steps).wait()
 
     own = row_block(me)
     for step in range(steps):
         target = groups - 1 - step
         for stream in (near, 1 - near):
             place = place_in(stream)
-            for k in range(kinds):
+            for chunk in range(chunks):
+                k, piece = chunk // pieces, chunk % pieces
 
                 @pl.when((place > 0) & (place <= target))
-                def _(stream=stream, place=place, k=k):
-                    slot = held[k].at[stream, step]
-                    copy = sum_copy(stream, step, k, slot)
+                def _(stream=stream, place=place, k=k, piece=piece, chunk=chunk):
+                    slot = slot_of(stream, step, chunk)
+                    copy = sum_copy(stream, step, chunk, slot)
                     copy.wait_recv()
 
                     @pl.when(place < target)
                     def _():
-                        slot[...] += x[k][row_block(wanted(stream, step))]
+                        slot[...] += x[k][piece_of(wanted(stream, step), piece)]
                         copy.start()
 
                     @pl.when(place == target)
                     def _():
-                        x[k][own] += slot[...]
+                        x[k][piece_of(me, piece)] += slot[...]
 
     group_tiles[me] = squares_tile(x[0][own]) + squares_tile(x[1][own])
     tile_copies = [
@@ -194,11 +221,6 @@
     limit = jnp.sqrt(jnp.full((1, 1), count, jnp.float32))
     clip = jnp.minimum(jnp.float32(1.0), limit / (jnp.sqrt(squares) + 1e-06))
 
-    height = rows // pieces
-
-    def piece_of(source_group, piece):
-        return pl.ds(pl.multiple_of(source_group * rows + piece * height, height), height)
-
     def gather_copy(stream, distance, chunk, source_group):
         k, piece = chunk // pieces, chunk % pieces
         block = gathered[k].at[piece_of(source_group, piece)]
@@ -221,7 +243,6 @@
     def has_next(stream):
         return me < groups - 1 if stream == 0 else me > 0
 
-    chunks = kinds * pieces
     stores = []
     for chunk in range(chunks):
         k, piece = chunk // pieces, chunk % pieces
@@ -234,6 +255,8 @@
 
             @pl.when(has_next(stream))
             def _(stream=stream):
+                if chunk >= 2:
+                    gather_copy(stream, 0, chunk - 2, me).wait_send()
                 gather_copy(stream, 0, chunk, me).start()
 
         p[part], m[part], v[part] = master, moment, variance
@@ -264,7 +287,7 @@
                     weight_store(stream, distance, chunk, origin).start()
 
     for distance in range(groups - 1):
-        for chunk in range(chunks):
+        for chunk in range(0 if distance else chunks - 2, chunks):
             for stream in range(2):
                 origin = me - distance if stream == 0 else me + distance
 
@@ -287,11 +310,11 @@
         target = groups - 1 - step
         for stream in (near, 1 - near):
             place = place_in(stream)
-            for k in range(kinds):
+            for chunk in range(chunks):
 
                 @pl.when((place > 0) & (place < target))
-                def _(stream=stream, k=k):
-                    sum_copy(stream, step, k, held[k].at[stream, step]).wait_send()
+                def _(stream=stream, chunk=chunk):
+                    sum_copy(stream, step, chunk, slot_of(stream, step, chunk)).wait_send()
 
     for copy in tile_copies + shard_copies:
         copy.wait_send()
@@ -349,8 +372,8 @@
         + [pltpu.VMEM((rows, w), f32) for w in widths] * 3
         + [pltpu.VMEM((full, w), bf16) for w in widths]
         + [pltpu.VMEM((groups, 8, 128), f32), pltpu.VMEM((shards, 8, 128), f32)]
-        + [dma((2,)), dma((2, 3)), dma((chunks, 3)), dma((2, groups, chunks))]
-        + [dma((2, groups - 1, 2))] * 2
+        + [dma((groups, 2)), dma((2, 3)), dma((chunks, 3)), dma((2, groups, chunks))]
+        + [dma((2, groups - 1, chunks))] * 2
         + [dma((groups,))] * 2
         + [dma((shards,))] * 2
         + [dma((2, groups, chunks))] * 2

time: 78.7 us -> 77.8 us (0.989)
  Pallas kernels: 77.9 us -> 77 us
    pallas_call x1, Pallas kernels: 75.1 us -> 74.2 us  [body(): pl.pallas_call(functools.partial(kernel, groups, shards, float(count), pi...]
where the time goes in v4:
time: 77.8 us; the launch traced here: 77.7 us
  Pallas kernels  77 us (99%)
    pallas_call x1, Pallas kernels, body(): pl.pallas_call(functools.partial(kernel, groups, shards, float(count), pi...  74.2 us
    pallas_call x1, Pallas kernels, copy_out(): pl.pallas_call(copy_kernel, out_shape=[jax.ShapeDtypeStruct(a.shape, a.dt...  2.78 us

profile of v4, /device:TPU:0, one launch (start us, length us, event | category | flops | bytes accessed | tf_op | source)
XLA Modules:
  0.0 77.7 jit_solution(6772526773482235090)
XLA Ops:
  0.6 74.2 %shard_map.143 = (f32[64,1280]{1,0:T(8,128)}, f32[64,1024]{1,0:T(8,128)}, f32[64,1280]{1,0:T(8,128)}, f32[64,1024]{1,0:T(8,128)}, f32[64,1280]{1,0:T(8,128)}, /*...) custom-call(f32[256,1280]{1,0:T(8,128)} %bitcast.16, f32[256,1024]{1,0:T(8,128)} %bitcast.17, ...), custom_call_target="tpu_custom_call" | custom-call | tf_op jit(solution)/shard_map/pallas_call | solution.py:381
  74.9 2.8 %shard_map.144 = (f32[64,1280]{1,0:T(8,128)}, f32[64,1024]{1,0:T(8,128)}, f32[64,1280]{1,0:T(8,128)}, f32[64,1024]{1,0:T(8,128)}, f32[64,1280]{1,0:T(8,128)}, /*...) custom-call(f32[64,1280]{1,0:T(8,128)} %get-tuple-element.24.refs_0_, ...), custom_call_target="tpu_custom_call" | custom-call | bytes 5898240 | tf_op jit(solution)/shard_map/pallas_call | solution.py:342

commit v5 on v4

--- a/solution.py
+++ b/solution.py
@@ -135,89 +135,208 @@
             device_id_type=MESH,
         )
 
-    @pl.when((me == 0) | (me == groups - 1))
-    def _():
-        copies = []
+    if groups == 4:
+        is_end = (me == 0) | (me == 3)
+        mirror = me // 2
+        total = 2 * chunks
+
+        def block(j):
+            return j + mirror * (3 - 2 * j)
+
+        inwards = {"group": me + 1 - 2 * mirror}
+        outwards = {"group": me - 1 + 2 * mirror}
+
+        def line_copy(source, send, lane, step, chunk, peer):
+            return pltpu.make_async_remote_copy(
+                src_ref=source,
+                dst_ref=slot_of(lane, step, chunk),
+                send_sem=sum_send.at[send, step, chunk],
+                recv_sem=sum_recv.at[lane, step, chunk],
+                device_id=peer,
+                device_id_type=MESH,
+            )
+
+        def end_copy(n):
+            step, chunk = n // chunks, n % chunks
+            source = x[chunk // pieces].at[piece_of(block(3 - step), chunk % pieces)]
+            return line_copy(source, 0, 0, step, chunk, inwards)
+
+        def across_copy(n):
+            step, chunk = n // chunks, n % chunks
+            return line_copy(slot_of(0, step, chunk), 0, 1, step, chunk, inwards)
+
+        def back_copy(n):
+            step, chunk = n // chunks, n % chunks
+            return line_copy(slot_of(1, step, chunk), 1, 1, step, chunk, outwards)
+
+        def shard_copy(offset):
+            return pltpu.make_async_remote_copy(
+                src_ref=shard_tiles.at[shard],
+                dst_ref=shard_tiles.at[shard],
+                send_sem=shard_send.at[offset],
+                recv_sem=shard_recv.at[offset],
+                device_id={"shard": lax.rem(shard + offset, shards)},
+                device_id_type=MESH,
+            )
+
+        def tile_copy(offset):
+            return pltpu.make_async_remote_copy(
+                src_ref=group_tiles.at[me],
+                dst_ref=group_tiles.at[me],
+                send_sem=tile_send.at[offset],
+                recv_sem=tile_recv.at[offset],
+                device_id={"group": lax.rem(me + offset, groups)},
+                device_id_type=MESH,
+            )
+
+        @pl.when(is_end)
+        def _():
+            lag = 6
+            shard_tiles[shard] = jnp.zeros((8, 128), jnp.float32)
+            for n in range(total + max(chunks, lag)):
+                if n == 0:
+                    load(0, 0).wait()
+                if n == 1:
+                    for step in range(groups):
+                        for k in range(kinds):
+                            if (step, k) != (0, 0):
+                                load(k, step).wait()
+                if n < total + chunks:
+                    if n >= 2:
+                        end_copy(n - 2).wait_send()
+                    end_copy(n).start()
+                m = n - lag
+                if 0 <= m < total:
+                    step, chunk = m // chunks, m % chunks
+                    k, place = chunk // pieces, piece_of(block(step), chunk % pieces)
+                    back_copy(m).wait_recv()
+                    summed = x[k][place] + slot_of(1, step, chunk)[...]
+                    if step == 0:
+                        x[k][place] = summed
+                    shard_tiles[shard] += squares_tile(summed)
+                if m == total - 1:
+                    for offset in range(1, shards):
+                        shard_copy(offset).start()
+            for offset in range(1, shards):
+                shard_copy(offset).wait_recv()
+            group_tiles[me] = jnp.sum(shard_tiles[...], axis=0)
+            for offset in range(1, groups):
+                tile_copy(offset).start()
+
+        @pl.when(jnp.logical_not(is_end))
+        def _():
+            for step in range(groups):
+                for k in range(kinds):
+                    load(k, step).wait()
+            for n in range(total + 1):
+                if n < total:
+                    step, chunk = n // chunks, n % chunks
+                    k, place = chunk // pieces, piece_of(block(3 - step), chunk % pieces)
+                    end_copy(n).wait_recv()
+                    slot_of(0, step, chunk)[...] += x[k][place]
+                    across_copy(n).start()
+                if n >= 1:
+                    step, chunk = (n - 1) // chunks, (n - 1) % chunks
+                    k, place = chunk // pieces, piece_of(block(step), chunk % pieces)
+                    across_copy(n - 1).wait_recv()
+                    slot_of(1, step, chunk)[...] += x[k][place]
+                    back_copy(n - 1).start()
+
+        for copy in state_loads:
+            copy.wait()
+        for source in (0, 3):
+
+            @pl.when(me != source)
+            def _(source=source):
+                tile_copy(lax.rem(me - source + groups, groups)).wait_recv()
+
+        norm_tiles = jnp.stack([group_tiles[0], group_tiles[3]])
+    else:
+        @pl.when((me == 0) | (me == groups - 1))
+        def _():
+            copies = []
+            for step in range(steps):
+                for chunk in range(chunks):
+                    k, piece = chunk // pieces, chunk % pieces
+                    if piece == 0:
+                        load(k, step).wait()
+                    source = x[k].at[piece_of(wanted(near, step), piece)]
+                    copies.append(sum_copy(near, step, chunk, source))
+                    if len(copies) > 2:
+                        copies[-3].wait_send()
+                    copies[-1].start()
+            for copy in copies[-2:]:
+                copy.wait_send()
+
+        @pl.when((me > 0) & (me < groups - 1))
+        def _():
+            for step in range(steps):
+                for k in range(kinds):
+                    load(k, step).wait()
+
+        for k in range(kinds):
+            load(k, steps).wait()
+
+        own = row_block(me)
         for step in range(steps):
-            for chunk in range(chunks):
-                k, piece = chunk // pieces, chunk % pieces
-                if piece == 0:
-                    load(k, step).wait()
-                source = x[k].at[piece_of(wanted(near, step), piece)]
-                copies.append(sum_copy(near, step, chunk, source))
-                if len(copies) > 2:
-                    copies[-3].wait_send()
-                copies[-1].start()
-        for copy in copies[-2:]:
-            copy.wait_send()
-
-    @pl.when((me > 0) & (me < groups - 1))
-    def _():
-        for step in range(steps):
-            for k in range(kinds):
-                load(k, step).wait()
-
-    for k in range(kinds):
-        load(k, steps).wait()
-
-    own = row_block(me)
-    for step in range(steps):
-        target = groups - 1 - step
-        for stream in (near, 1 - near):
-            place = place_in(stream)
-            for chunk in range(chunks):
-                k, piece = chunk // pieces, chunk % pieces
-
-                @pl.when((place > 0) & (place <= target))
-                def _(stream=stream, place=place, k=k, piece=piece, chunk=chunk):
-                    slot = slot_of(stream, step, chunk)
-                    copy = sum_copy(stream, step, chunk, slot)
-                    copy.wait_recv()
-
-                    @pl.when(place < target)
-                    def _():
-                        slot[...] += x[k][piece_of(wanted(stream, step), piece)]
-                        copy.start()
-
-                    @pl.when(place == target)
-                    def _():
-                        x[k][piece_of(me, piece)] += slot[...]
-
-    group_tiles[me] = squares_tile(x[0][own]) + squares_tile(x[1][own])
-    tile_copies = [
-        pltpu.make_async_remote_copy(
-            src_ref=group_tiles.at[me],
-            dst_ref=group_tiles.at[me],
-            send_sem=tile_send.at[offset],
-            recv_sem=tile_recv.at[offset],
-            device_id={"group": lax.rem(me + offset, groups)},
-            device_id_type=MESH,
-        )
-        for offset in range(1, groups)
-    ]
-    for copy in tile_copies:
-        copy.start()
-    for copy in state_loads:
-        copy.wait()
-    for copy in tile_copies:
-        copy.wait_recv()
-    shard_tiles[shard] = jnp.sum(group_tiles[...], axis=0)
-    shard_copies = [
-        pltpu.make_async_remote_copy(
-            src_ref=shard_tiles.at[shard],
-            dst_ref=shard_tiles.at[shard],
-            send_sem=shard_send.at[offset],
-            recv_sem=shard_recv.at[offset],
-            device_id={"shard": lax.rem(shard + offset, shards)},
-            device_id_type=MESH,
-        )
-        for offset in range(1, shards)
-    ]
-    for copy in shard_copies:
-        copy.start()
-    for copy in shard_copies:
-        copy.wait_recv()
-    squares = jnp.sum(jnp.sum(shard_tiles[...], axis=0), keepdims=True)
+            target = groups - 1 - step
+            for stream in (near, 1 - near):
+                place = place_in(stream)
+                for chunk in range(chunks):
+                    k, piece = chunk // pieces, chunk % pieces
+
+                    @pl.when((place > 0) & (place <= target))
+                    def _(stream=stream, place=place, k=k, piece=piece, chunk=chunk):
+                        slot = slot_of(stream, step, chunk)
+                        copy = sum_copy(stream, step, chunk, slot)
+                        copy.wait_recv()
+
+                        @pl.when(place < target)
+                        def _():
+                            slot[...] += x[k][piece_of(wanted(stream, step), piece)]
+                            copy.start()
+
+                        @pl.when(place == target)
+                        def _():
+                            x[k][piece_of(me, piece)] += slot[...]
+
+        group_tiles[me] = squares_tile(x[0][own]) + squares_tile(x[1][own])
+        tile_copies = [
+            pltpu.make_async_remote_copy(
+                src_ref=group_tiles.at[me],
+                dst_ref=group_tiles.at[me],
+                send_sem=tile_send.at[offset],
+                recv_sem=tile_recv.at[offset],
+                device_id={"group": lax.rem(me + offset, groups)},
+                device_id_type=MESH,
+            )
+            for offset in range(1, groups)
+        ]
+        for copy in tile_copies:
+            copy.start()
+        for copy in tile_copies:
+            copy.wait_recv()
+        shard_tiles[shard] = jnp.sum(group_tiles[...], axis=0)
+        shard_copies = [
+            pltpu.make_async_remote_copy(
+                src_ref=shard_tiles.at[shard],
+                dst_ref=shard_tiles.at[shard],
+                send_sem=shard_send.at[offset],
+                recv_sem=shard_recv.at[offset],
+                device_id={"shard": lax.rem(shard + offset, shards)},
+                device_id_type=MESH,
+            )
+            for offset in range(1, shards)
+        ]
+        for copy in shard_copies:
+            copy.start()
+        for copy in shard_copies:
+            copy.wait_recv()
+        norm_tiles = shard_tiles[...]
+        for copy in state_loads:
+            copy.wait()
+
+    squares = jnp.sum(jnp.sum(norm_tiles, axis=0), keepdims=True)
     limit = jnp.sqrt(jnp.full((1, 1), count, jnp.float32))
     clip = jnp.minimum(jnp.float32(1.0), limit / (jnp.sqrt(squares) + 1e-06))
 
@@ -249,14 +368,21 @@
         part = slice(piece * height, (piece + 1) * height)
         p, m, v = states[k]
         at = piece_of(me, piece)
+        if groups == 4:
+
+            @pl.when(jnp.logical_not(is_end))
+            def _():
+                end_copy(total + chunk).wait_recv()
+                x[k][at] = slot_of(1, 1, chunk)[...] + slot_of(0, 2, chunk)[...]
+
         master, moment, variance = adamw_step(p[part], m[part], v[part], x[k][at], clip)
         gathered[k][at] = master.astype(jnp.bfloat16)
         for stream in range(2):
 
             @pl.when(has_next(stream))
             def _(stream=stream):
-                if chunk >= 2:
-                    gather_copy(stream, 0, chunk - 2, me).wait_send()
+                if chunk >= 3:
+                    gather_copy(stream, 0, chunk - 3, me).wait_send()
                 gather_copy(stream, 0, chunk, me).start()
 
         p[part], m[part], v[part] = master, moment, variance
@@ -287,7 +413,7 @@
                     weight_store(stream, distance, chunk, origin).start()
 
     for distance in range(groups - 1):
-        for chunk in range(0 if distance else chunks - 2, chunks):
+        for chunk in range(0 if distance else max(0, chunks - 3), chunks):
             for stream in range(2):
                 origin = me - distance if stream == 0 else me + distance
 
@@ -306,18 +432,36 @@
                 def _(stream=stream, origin=origin):
                     weight_store(stream, distance, chunk, origin).wait()
 
-    for step in range(steps):
-        target = groups - 1 - step
-        for stream in (near, 1 - near):
-            place = place_in(stream)
-            for chunk in range(chunks):
-
-                @pl.when((place > 0) & (place < target))
-                def _(stream=stream, chunk=chunk):
-                    sum_copy(stream, step, chunk, slot_of(stream, step, chunk)).wait_send()
-
-    for copy in tile_copies + shard_copies:
-        copy.wait_send()
+    if groups == 4:
+
+        @pl.when(is_end)
+        def _():
+            for n in range(total + chunks - 2, total + chunks):
+                end_copy(n).wait_send()
+            for offset in range(1, shards):
+                shard_copy(offset).wait_send()
+            for offset in range(1, groups):
+                tile_copy(offset).wait_send()
+
+        @pl.when(jnp.logical_not(is_end))
+        def _():
+            for n in range(total):
+                across_copy(n).wait_send()
+                back_copy(n).wait_send()
+
+    else:
+        for step in range(steps):
+            target = groups - 1 - step
+            for stream in (near, 1 - near):
+                place = place_in(stream)
+                for chunk in range(chunks):
+
+                    @pl.when((place > 0) & (place < target))
+                    def _(stream=stream, chunk=chunk):
+                        sum_copy(stream, step, chunk, slot_of(stream, step, chunk)).wait_send()
+
+        for copy in tile_copies + shard_copies:
+            copy.wait_send()
     for copy in stores:
         copy.wait()
 
@@ -356,7 +500,7 @@
     full, entry_width = entry_grads.shape[2:]
     exit_width = exit_grads.shape[3]
     rows = full // groups
-    pieces = max(1, rows // 32)
+    pieces = max(1, rows // 16)
     count = full * (entry_width + exit_width) * shards
     widths = (entry_width, exit_width)
     f32, bf16 = jnp.float32, jnp.bfloat16

time: 77.8 us -> 79.2 us (1.018)
  Pallas kernels: 77 us -> 78.4 us
    pallas_call x1, Pallas kernels: 74.2 us -> 75.6 us  [body(): pl.pallas_call(functools.partial(kernel, groups, shards, float(count), pi...]
where the time goes in v5:
time: 79.2 us; the launch traced here: 79 us
  Pallas kernels  78.4 us (99%)
    pallas_call x1, Pallas kernels, body(): pl.pallas_call(functools.partial(kernel, groups, shards, float(count), pi...  75.6 us
    pallas_call x1, Pallas kernels, copy_out(): pl.pallas_call(copy_kernel, out_shape=[jax.ShapeDtypeStruct(a.shape, a.dt...  2.78 us

profile of v5, /device:TPU:0, one launch (start us, length us, event | category | flops | bytes accessed | tf_op | source)
XLA Modules:
  0.0 79.0 jit_solution(869973833615486741)
XLA Ops:
  0.6 75.6 %shard_map.143 = (f32[64,1280]{1,0:T(8,128)}, f32[64,1024]{1,0:T(8,128)}, f32[64,1280]{1,0:T(8,128)}, f32[64,1024]{1,0:T(8,128)}, f32[64,1280]{1,0:T(8,128)}, /*...) custom-call(f32[256,1280]{1,0:T(8,128)} %bitcast.16, f32[256,1024]{1,0:T(8,128)} %bitcast.17, ...), custom_call_target="tpu_custom_call" | custom-call | tf_op jit(solution)/shard_map/pallas_call | solution.py:525
  76.2 2.8 %shard_map.144 = (f32[64,1280]{1,0:T(8,128)}, f32[64,1024]{1,0:T(8,128)}, f32[64,1280]{1,0:T(8,128)}, f32[64,1024]{1,0:T(8,128)}, f32[64,1280]{1,0:T(8,128)}, /*...) custom-call(f32[64,1280]{1,0:T(8,128)} %get-tuple-element.24.refs_0_, ...), custom_call_target="tpu_custom_call" | custom-call | bytes 5898240 | tf_op jit(solution)/shard_map/pallas_call | solution.py:486

commit v6 on v5

--- a/solution.py
+++ b/solution.py
@@ -51,7 +51,7 @@
     entry_x, exit_x, entry_held, exit_held,
     entry_p, exit_p, entry_m, exit_m, entry_v, exit_v, entry_w, exit_w,
     group_tiles, shard_tiles,
-    load_sem, state_sem, store_sem, weight_sem,
+    load_sem, state_sem, store_sem,
     sum_send, sum_recv, tile_send, tile_recv, shard_send, shard_recv,
     gather_send, gather_recv,
 ):
@@ -191,7 +191,7 @@
 
         @pl.when(is_end)
         def _():
-            lag = 6
+            lag = 8
             shard_tiles[shard] = jnp.zeros((8, 128), jnp.float32)
             for n in range(total + max(chunks, lag)):
                 if n == 0:
@@ -340,80 +340,78 @@
     limit = jnp.sqrt(jnp.full((1, 1), count, jnp.float32))
     clip = jnp.minimum(jnp.float32(1.0), limit / (jnp.sqrt(squares) + 1e-06))
 
-    def gather_copy(stream, distance, chunk, source_group):
-        k, piece = chunk // pieces, chunk % pieces
-        block = gathered[k].at[piece_of(source_group, piece)]
+    parts = max(1, pieces // 2)
+    tall = rows // parts
+    batches = kinds * parts
+    sums_in_batch = pieces // parts
+
+    def gather_copy(stream, distance, batch, source_group):
+        k, part = batch // parts, batch % parts
+        place = pl.ds(pl.multiple_of(source_group * rows + part * tall, tall), tall)
         return pltpu.make_async_remote_copy(
-            src_ref=block,
-            dst_ref=block,
-            send_sem=gather_send.at[stream, distance, chunk],
-            recv_sem=gather_recv.at[stream, distance, chunk],
+            src_ref=gathered[k].at[place],
+            dst_ref=gathered[k].at[place],
+            send_sem=gather_send.at[stream, distance, batch],
+            recv_sem=gather_recv.at[stream, distance, batch],
             device_id=peer_in(stream),
             device_id_type=MESH,
         )
 
-    def weight_store(stream, distance, chunk, source_group):
-        k, piece = chunk // pieces, chunk % pieces
-        place = piece_of(source_group, piece)
-        return pltpu.make_async_copy(
-            gathered[k].at[place], weights[k].at[place], weight_sem.at[stream, distance, chunk]
-        )
-
     def has_next(stream):
         return me < groups - 1 if stream == 0 else me > 0
 
-    stores = []
-    for chunk in range(chunks):
-        k, piece = chunk // pieces, chunk % pieces
-        part = slice(piece * height, (piece + 1) * height)
+    for batch in range(batches):
+        k, part = batch // parts, batch % parts
+        rows_in = slice(part * tall, (part + 1) * tall)
         p, m, v = states[k]
-        at = piece_of(me, piece)
+        at = pl.ds(pl.multiple_of(me * rows + part * tall, tall), tall)
         if groups == 4:
 
             @pl.when(jnp.logical_not(is_end))
             def _():
-                end_copy(total + chunk).wait_recv()
-                x[k][at] = slot_of(1, 1, chunk)[...] + slot_of(0, 2, chunk)[...]
-
-        master, moment, variance = adamw_step(p[part], m[part], v[part], x[k][at], clip)
+                for chunk in range(batch * sums_in_batch, (batch + 1) * sums_in_batch):
+                    end_copy(total + chunk).wait_recv()
+                    x[k][piece_of(me, chunk % pieces)] = (
+                        slot_of(1, 1, chunk)[...] + slot_of(0, 2, chunk)[...]
+                    )
+
+        master, moment, variance = adamw_step(p[rows_in], m[rows_in], v[rows_in], x[k][at], clip)
         gathered[k][at] = master.astype(jnp.bfloat16)
         for stream in range(2):
 
             @pl.when(has_next(stream))
             def _(stream=stream):
-                if chunk >= 3:
-                    gather_copy(stream, 0, chunk - 3, me).wait_send()
-                gather_copy(stream, 0, chunk, me).start()
-
-        p[part], m[part], v[part] = master, moment, variance
-        copies = [weight_store(0, 0, chunk, me)]
-        for i in range(3):
-            copies.append(
-                pltpu.make_async_copy(
-                    states[k][i].at[part], state_out[k][i].at[part], store_sem.at[chunk, i]
-                )
-            )
-        for copy in copies:
-            copy.start()
-        stores += copies
+                gather_copy(stream, 0, batch, me).start()
+
+        p[rows_in], m[rows_in], v[rows_in] = master, moment, variance
+
+    stores = [
+        pltpu.make_async_copy(states[k][i], state_out[k][i], store_sem.at[k, i])
+        for k in range(kinds)
+        for i in range(3)
+    ]
+    for copy in stores:
+        copy.start()
 
     for distance in range(1, groups):
-        for chunk in range(chunks):
+        for batch in range(batches):
             for stream in range(2):
                 origin = me - distance if stream == 0 else me + distance
 
                 @pl.when(origin >= 0 if stream == 0 else origin < groups)
                 def _(stream=stream, origin=origin):
-                    gather_copy(stream, distance - 1, chunk, origin).wait_recv()
+                    gather_copy(stream, distance - 1, batch, origin).wait_recv()
 
                     @pl.when(has_next(stream))
                     def _():
-                        gather_copy(stream, distance, chunk, origin).start()
-
-                    weight_store(stream, distance, chunk, origin).start()
+                        gather_copy(stream, distance, batch, origin).start()
+
+    for k in range(kinds):
+        stores.append(pltpu.make_async_copy(gathered[k], weights[k], store_sem.at[k, 3]))
+        stores[-1].start()
 
     for distance in range(groups - 1):
-        for chunk in range(0 if distance else max(0, chunks - 3), chunks):
+        for batch in range(batches):
             for stream in range(2):
                 origin = me - distance if stream == 0 else me + distance
 
@@ -421,16 +419,7 @@
                     has_next(stream) & (origin >= 0 if stream == 0 else origin < groups)
                 )
                 def _(stream=stream, origin=origin):
-                    gather_copy(stream, distance, chunk, origin).wait_send()
-
-    for distance in range(1, groups):
-        for chunk in range(chunks):
-            for stream in range(2):
-                origin = me - distance if stream == 0 else me + distance
-
-                @pl.when(origin >= 0 if stream == 0 else origin < groups)
-                def _(stream=stream, origin=origin):
-                    weight_store(stream, distance, chunk, origin).wait()
+                    gather_copy(stream, distance, batch, origin).wait_send()
 
     if groups == 4:
 
@@ -516,7 +505,7 @@
         + [pltpu.VMEM((rows, w), f32) for w in widths] * 3
         + [pltpu.VMEM((full, w), bf16) for w in widths]
         + [pltpu.VMEM((groups, 8, 128), f32), pltpu.VMEM((shards, 8, 128), f32)]
-        + [dma((groups, 2)), dma((2, 3)), dma((chunks, 3)), dma((2, groups, chunks))]
+        + [dma((groups, 2)), dma((2, 3)), dma((2, 4))]
         + [dma((2, groups - 1, chunks))] * 2
         + [dma((groups,))] * 2
         + [dma((shards,))] * 2

time: 79.2 us -> 78.7 us (level)
  no operation moved by 1% of the time
where the time goes in v6:
time: 78.7 us; the launch traced here: 78.5 us
  Pallas kernels  77.9 us (99%)
    pallas_call x1, Pallas kernels, body(): pl.pallas_call(functools.partial(kernel, groups, shards, float(count), pi...  75.1 us
    pallas_call x1, Pallas kernels, copy_out(): pl.pallas_call(copy_kernel, out_shape=[jax.ShapeDtypeStruct(a.shape, a.dt...  2.78 us

profile of v6, /device:TPU:0, one launch (start us, length us, event | category | flops | bytes accessed | tf_op | source)
XLA Modules:
  0.0 78.5 jit_solution(13843608068078988532)
XLA Ops:
  0.6 75.1 %shard_map.143 = (f32[64,1280]{1,0:T(8,128)}, f32[64,1024]{1,0:T(8,128)}, f32[64,1280]{1,0:T(8,128)}, f32[64,1024]{1,0:T(8,128)}, f32[64,1280]{1,0:T(8,128)}, /*...) custom-call(f32[256,1280]{1,0:T(8,128)} %bitcast.16, f32[256,1024]{1,0:T(8,128)} %bitcast.17, ...), custom_call_target="tpu_custom_call" | custom-call | tf_op jit(solution)/shard_map/pallas_call | solution.py:514
  75.7 2.8 %shard_map.144 = (f32[64,1280]{1,0:T(8,128)}, f32[64,1024]{1,0:T(8,128)}, f32[64,1280]{1,0:T(8,128)}, f32[64,1024]{1,0:T(8,128)}, f32[64,1280]{1,0:T(8,128)}, /*...) custom-call(f32[64,1280]{1,0:T(8,128)} %get-tuple-element.24.refs_0_, ...), custom_call_target="tpu_custom_call" | custom-call | bytes 5898240 | tf_op jit(solution)/shard_map/pallas_call | solution.py:475

commit v7 on v6

--- a/solution.py
+++ b/solution.py
@@ -139,6 +139,7 @@
         is_end = (me == 0) | (me == 3)
         mirror = me // 2
         total = 2 * chunks
+        window = min(6, chunks)
 
         def block(j):
             return j + mirror * (3 - 2 * j)
@@ -202,8 +203,8 @@
                             if (step, k) != (0, 0):
                                 load(k, step).wait()
                 if n < total + chunks:
-                    if n >= 2:
-                        end_copy(n - 2).wait_send()
+                    if n >= window:
+                        end_copy(n - window).wait_send()
                     end_copy(n).start()
                 m = n - lag
                 if 0 <= m < total:
@@ -425,7 +426,7 @@
 
         @pl.when(is_end)
         def _():
-            for n in range(total + chunks - 2, total + chunks):
+            for n in range(total + chunks - window, total + chunks):
                 end_copy(n).wait_send()
             for offset in range(1, shards):
                 shard_copy(offset).wait_send()

time: 78.7 us -> 78.7 us (level)
  no operation moved by 1% of the time
where the time goes in v7:
time: 78.7 us; the launch traced here: 78.5 us
  Pallas kernels  77.9 us (99%)
    pallas_call x1, Pallas kernels, body(): pl.pallas_call(functools.partial(kernel, groups, shards, float(count), pi...  75.1 us
    pallas_call x1, Pallas kernels, copy_out(): pl.pallas_call(copy_kernel, out_shape=[jax.ShapeDtypeStruct(a.shape, a.dt...  2.78 us

profile of v7, /device:TPU:0, one launch (start us, length us, event | category | flops | bytes accessed | tf_op | source)
XLA Modules:
  0.0 78.5 jit_solution(7965413985450551190)
XLA Ops:
  0.6 75.1 %shard_map.143 = (f32[64,1280]{1,0:T(8,128)}, f32[64,1024]{1,0:T(8,128)}, f32[64,1280]{1,0:T(8,128)}, f32[64,1024]{1,0:T(8,128)}, f32[64,1280]{1,0:T(8,128)}, /*...) custom-call(f32[256,1280]{1,0:T(8,128)} %bitcast.16, f32[256,1024]{1,0:T(8,128)} %bitcast.17, ...), custom_call_target="tpu_custom_call" | custom-call | tf_op jit(solution)/shard_map/pallas_call | solution.py:515
  75.7 2.8 %shard_map.144 = (f32[64,1280]{1,0:T(8,128)}, f32[64,1024]{1,0:T(8,128)}, f32[64,1280]{1,0:T(8,128)}, f32[64,1024]{1,0:T(8,128)}, f32[64,1280]{1,0:T(8,128)}, /*...) custom-call(f32[64,1280]{1,0:T(8,128)} %get-tuple-element.24.refs_0_, ...), custom_call_target="tpu_custom_call" | custom-call | bytes 5898240 | tf_op jit(solution)/shard_map/pallas_call | solution.py:476

commit v8 on v4

--- a/solution.py
+++ b/solution.py
@@ -51,7 +51,7 @@
     entry_x, exit_x, entry_held, exit_held,
     entry_p, exit_p, entry_m, exit_m, entry_v, exit_v, entry_w, exit_w,
     group_tiles, shard_tiles,
-    load_sem, state_sem, store_sem, weight_sem,
+    load_sem, state_sem, store_sem,
     sum_send, sum_recv, tile_send, tile_recv, shard_send, shard_recv,
     gather_send, gather_recv,
 ):
@@ -233,17 +233,9 @@
             device_id_type=MESH,
         )
 
-    def weight_store(stream, distance, chunk, source_group):
-        k, piece = chunk // pieces, chunk % pieces
-        place = piece_of(source_group, piece)
-        return pltpu.make_async_copy(
-            gathered[k].at[place], weights[k].at[place], weight_sem.at[stream, distance, chunk]
-        )
-
     def has_next(stream):
         return me < groups - 1 if stream == 0 else me > 0
 
-    stores = []
     for chunk in range(chunks):
         k, piece = chunk // pieces, chunk % pieces
         part = slice(piece * height, (piece + 1) * height)
@@ -260,16 +252,14 @@
                 gather_copy(stream, 0, chunk, me).start()
 
         p[part], m[part], v[part] = master, moment, variance
-        copies = [weight_store(0, 0, chunk, me)]
-        for i in range(3):
-            copies.append(
-                pltpu.make_async_copy(
-                    states[k][i].at[part], state_out[k][i].at[part], store_sem.at[chunk, i]
-                )
-            )
-        for copy in copies:
-            copy.start()
-        stores += copies
+
+    stores = [
+        pltpu.make_async_copy(states[k][i], state_out[k][i], store_sem.at[k, i])
+        for k in range(kinds)
+        for i in range(3)
+    ]
+    for copy in stores:
+        copy.start()
 
     for distance in range(1, groups):
         for chunk in range(chunks):
@@ -284,7 +274,9 @@
                     def _():
                         gather_copy(stream, distance, chunk, origin).start()
 
-                    weight_store(stream, distance, chunk, origin).start()
+    for k in range(kinds):
+        stores.append(pltpu.make_async_copy(gathered[k], weights[k], store_sem.at[k, 3]))
+        stores[-1].start()
 
     for distance in range(groups - 1):
         for chunk in range(0 if distance else chunks - 2, chunks):
@@ -296,15 +288,6 @@
                 )
                 def _(stream=stream, origin=origin):
                     gather_copy(stream, distance, chunk, origin).wait_send()
-
-    for distance in range(1, groups):
-        for chunk in range(chunks):
-            for stream in range(2):
-                origin = me - distance if stream == 0 else me + distance
-
-                @pl.when(origin >= 0 if stream == 0 else origin < groups)
-                def _(stream=stream, origin=origin):
-                    weight_store(stream, distance, chunk, origin).wait()
 
     for step in range(steps):
         target = groups - 1 - step
@@ -372,7 +355,7 @@
         + [pltpu.VMEM((rows, w), f32) for w in widths] * 3
         + [pltpu.VMEM((full, w), bf16) for w in widths]
         + [pltpu.VMEM((groups, 8, 128), f32), pltpu.VMEM((shards, 8, 128), f32)]
-        + [dma((groups, 2)), dma((2, 3)), dma((chunks, 3)), dma((2, groups, chunks))]
+        + [dma((groups, 2)), dma((2, 3)), dma((2, 4))]
         + [dma((2, groups - 1, chunks))] * 2
         + [dma((groups,))] * 2
         + [dma((shards,))] * 2

time: 77.8 us -> 77.8 us (level)
  no operation moved by 1% of the time
where the time goes in v8:
time: 77.8 us; the launch traced here: 77.7 us
  Pallas kernels  77 us (99%)
    pallas_call x1, Pallas kernels, body(): pl.pallas_call(functools.partial(kernel, groups, shards, float(count), pi...  74.3 us
    pallas_call x1, Pallas kernels, copy_out(): pl.pallas_call(copy_kernel, out_shape=[jax.ShapeDtypeStruct(a.shape, a.dt...  2.78 us

profile of v8, /device:TPU:0, one launch (start us, length us, event | category | flops | bytes accessed | tf_op | source)
XLA Modules:
  0.0 77.7 jit_solution(3720957775851980580)
XLA Ops:
  0.6 74.3 %shard_map.143 = (f32[64,1280]{1,0:T(8,128)}, f32[64,1024]{1,0:T(8,128)}, f32[64,1280]{1,0:T(8,128)}, f32[64,1024]{1,0:T(8,128)}, f32[64,1280]{1,0:T(8,128)}, /*...) custom-call(f32[256,1280]{1,0:T(8,128)} %bitcast.16, f32[256,1024]{1,0:T(8,128)} %bitcast.17, ...), custom_call_target="tpu_custom_call" | custom-call | tf_op jit(solution)/shard_map/pallas_call | solution.py:364
  74.9 2.8 %shard_map.144 = (f32[64,1280]{1,0:T(8,128)}, f32[64,1024]{1,0:T(8,128)}, f32[64,1280]{1,0:T(8,128)}, f32[64,1024]{1,0:T(8,128)}, f32[64,1280]{1,0:T(8,128)}, /*...) custom-call(f32[64,1280]{1,0:T(8,128)} %get-tuple-element.24.refs_0_, ...), custom_call_target="tpu_custom_call" | custom-call | bytes 5898240 | tf_op jit(solution)/shard_map/pallas_call | solution.py:325
